TPU v7x, 256 devices: a whole 4x4x8 slice. The times are simulated.
256 devices in a mesh: bulk: 16 (over x_lo, y, core), wide: 16 (over x_hi, z).
Axes of the slice: x: 4 (x_hi: 2, x_lo: 2; x = x_hi * 2 + x_lo), y: 4, z: 8, core: 2. Of those that a mesh axis runs over, the one named last changes fastest.
Arguments:
- eps_corr: bfloat16 [2, 12288, 49152], P(None, 'bulk', 'wide'), may hold values from -0.00036621094 to 0.00036621094
- pair_rows: bfloat16 [2, 96, 12288], P(None, None, ('bulk', 'wide')), may hold values from -6 to 6
- pair_cols: bfloat16 [2, 96, 49152], P(None, None, ('wide', 'bulk')), may hold values from -6 to 6
- coulomb: float32 [49152], P(('wide', 'bulk')), may hold values from 0.3 to 3
- wing_row: bfloat16 [2, 49152], P(None, ('wide', 'bulk')), may hold values from -0.02734375 to 0.02734375
- wing_col: bfloat16 [2, 12288], P(None, ('bulk', 'wide')), may hold values from -0.0546875 to 0.0546875
- pair_head: float32 [2, 96], replicated, may hold values from -6 to 6
- head_value: float32 [2], replicated, may hold values from -4 to 4
- head_coulomb: float32 [1], replicated, may hold values from 0.5 to 2
- inner_bands: int32 [12], replicated, may hold values from 0 to 23
Outputs:
- self_energy: float32 [2, 8, 8], replicated
All inputs are finite; a program needn't handle non-finite values.
Results may differ from a plain program's by a relative error of at most 0.002.
Values may be sent and summed in bfloat16 or wider, within the bound.
A program may use at most 64 MiB of HBM per device.

v0:
```python
import jax
import jax.numpy as jnp
from jax import lax
from jax.sharding import PartitionSpec as P

NT = 8
NL = 12
NVAL = 12


def pair_sum(left_re, left_im, right_re, right_im, weights):
    layout = (NT, NL, -1)
    left_re = left_re.reshape(layout)
    left_im = left_im.reshape(layout)
    scaled_re = right_re.reshape(layout) * weights[None, :, None]
    scaled_im = right_im.reshape(layout) * weights[None, :, None]
    pattern = "nlx,mlx->nm"
    highest = lax.Precision.HIGHEST
    real_part = jnp.einsum(pattern, left_re, scaled_re, precision=highest) - jnp.einsum(
        pattern, left_im, scaled_im, precision=highest
    )
    imag_part = jnp.einsum(pattern, left_re, scaled_im, precision=highest) + jnp.einsum(
        pattern, left_im, scaled_re, precision=highest
    )
    return jnp.stack([real_part, imag_part])


def local(
    eps_corr,
    pair_rows,
    pair_cols,
    coulomb,
    wing_row,
    wing_col,
    pair_head,
    head_value,
    head_coulomb,
    inner_bands,
):
    highest = lax.Precision.HIGHEST
    weights = jnp.where(inner_bands < NVAL, -0.5, 0.5).astype(jnp.float32)
    weighted = (coulomb[None, None, :] * pair_cols.astype(jnp.float32)).astype(jnp.bfloat16)
    weighted_local = weighted.astype(jnp.float32)
    rows_local = pair_rows.astype(jnp.float32)
    contract_last = (((1,), (1,)), ((), ()))
    portion = lax.all_gather(weighted, "bulk", axis=2, tiled=True)
    image_re = lax.dot_general(
        portion[0], eps_corr[0], contract_last, preferred_element_type=jnp.float32
    ) - lax.dot_general(portion[1], eps_corr[1], contract_last, preferred_element_type=jnp.float32)
    image_im = lax.dot_general(
        portion[0], eps_corr[1], contract_last, preferred_element_type=jnp.float32
    ) + lax.dot_general(portion[1], eps_corr[0], contract_last, preferred_element_type=jnp.float32)
    images = jnp.stack([image_re, image_im])
    shares = lax.psum_scatter(images, "wide", scatter_dimension=2, tiled=True)
    main_part = pair_sum(rows_local[0], -rows_local[1], shares[0], shares[1], weights)
    wing_cols = wing_row.astype(jnp.float32)
    gain_re = jnp.dot(weighted_local[0], wing_cols[0], precision=highest) - jnp.dot(
        weighted_local[1], wing_cols[1], precision=highest
    )
    gain_im = jnp.dot(weighted_local[0], wing_cols[1], precision=highest) + jnp.dot(
        weighted_local[1], wing_cols[0], precision=highest
    )
    row_wing = pair_sum(
        pair_head[0][:, None], -pair_head[1][:, None], gain_re[:, None], gain_im[:, None], weights
    )
    wing_rows = wing_col.astype(jnp.float32)
    tilt_re = jnp.dot(rows_local[0], wing_rows[0], precision=highest) + jnp.dot(
        rows_local[1], wing_rows[1], precision=highest
    )
    tilt_im = jnp.dot(rows_local[0], wing_rows[1], precision=highest) - jnp.dot(
        rows_local[1], wing_rows[0], precision=highest
    )
    coulomb_zero = head_coulomb[0]
    col_wing = pair_sum(
        tilt_re[:, None],
        tilt_im[:, None],
        coulomb_zero * pair_head[0][:, None],
        coulomb_zero * pair_head[1][:, None],
        weights,
    )
    wing_part = row_wing + col_wing
    summed = lax.psum(main_part, ("bulk", "wide")) + lax.psum(wing_part, ("bulk", "wide"))
    scaled_re = coulomb_zero * (head_value[0] * pair_head[0] - head_value[1] * pair_head[1])
    scaled_im = coulomb_zero * (head_value[0] * pair_head[1] + head_value[1] * pair_head[0])
    head_term = pair_sum(pair_head[0], -pair_head[1], scaled_re, scaled_im, weights)
    return summed + head_term


def solution(mesh):
    placed = (
        P(None, "bulk", "wide"),
        P(None, None, ("bulk", "wide")),
        P(None, None, ("wide", "bulk")),
        P(("wide", "bulk")),
        P(None, ("wide", "bulk")),
        P(None, ("bulk", "wide")),
        P(),
        P(),
        P(),
        P(),
    )
    return jax.shard_map(local, mesh=mesh, in_specs=placed, out_specs=P(), check_vma=False)
```

profile of v0, /device:TPU:1, one launch (start us, length us, event | category | flops | bytes accessed | tf_op | source)
XLA Modules:
  0.0 316.9 jit_solution(8514183984019851116)
XLA Ops:
  6.5 0.9 multiply_convert_fusion
  7.5 0.7 copy.79
  8.3 0.7 convert_negate_fusion
  9.0 0.7 slice.86
  9.7 0.8 convolution_bitcast_fusion.6
  10.5 0.8 convolution_bitcast_fusion.4
  11.3 0.7 compare_select_fusion
  12.2 0.1 copy.85
  12.4 0.8 fusion.37
  13.3 1.4 fusion.105
  15.3 2.0 multiply_reduce_fusion.1
  17.4 0.8 fusion.39
  18.4 0.1 fusion.106
  18.5 0.1 fusion.29
  18.8 0.1 fusion.107
  18.9 0.1 fusion.28
  19.2 0.8 convolution_bitcast_fusion.11
  20.0 0.8 fusion.35
  21.0 0.8 convolution_bitcast_fusion.9
  21.9 0.8 fusion.34
  22.9 0.1 fusion.62
  23.1 0.1 fusion.25
  23.3 0.1 fusion.58
  23.4 0.1 fusion.24
  23.6 1.3 dynamic-slice
  25.5 23.8 %all-gather.2.cloned.1.call-done = bf16[2,96,3072]{1,0,2:T(2,128)(2,1)} async-done(((bf16[2,96,192]{1,0,2:T(2,128)(2,1)}), bf16[2,96,3072]{1,0,2:T(2,128)(2,1)}) %all-gather.2.cloned.1.call-update) | async-done | bytes 1179664 | tf_op jit(solution)/shard_map/all_gather | solution.py:46
  49.3 4.4 %fusion.104 = (bf16[1,96,3072]{1,0,2:T(2,128)(2,1)S(1)}, bf16[1,96,3072]{1,0,2:T(2,128)(2,1)S(1)}) fusion(bf16[2,96,3072]{1,0,2:T(2,128)(2,1)} %all-gather.2.cloned.1.call-done), kind=kLoop, calls=%fused_computation.133 | loop fusion | bytes 2359296 | tf_op jit(solution)/shard_map/slice | solution.py:49
  53.7 2.9 copy.104
  56.6 1.6 copy.103
  58.1 4.1 %fusion.2 = f32[96,768]{1,0:T(8,128)S(1)} fusion(bf16[2,768,3072]{2,1,0:T(8,128)(2,1)} %param.10, bf16[1,96,3072]{2,1,0:T(8,128)(2,1)} %copy.104), kind=kOutput, calls=%fused_computation.2 | convolution fusion | flops 452984832 | bytes 5603328 | tf_op jit(solution)/shard_map/dot_general | solution.py:49
  62.3 3.9 %fusion = f32[96,768]{1,0:T(8,128)S(1)} fusion(bf16[2,768,3072]{2,1,0:T(8,128)(2,1)} %param.10, bf16[1,96,3072]{2,1,0:T(8,128)(2,1)S(1)} %copy.103), kind=kOutput, calls=%fused_computation | convolution fusion | flops 452984832 | bytes 5603328 | tf_op jit(solution)/shard_map/dot_general | solution.py:50
  66.2 4.0 %fusion.15 = f32[1,96,768]{2,1,0:T(8,128)S(1)} fusion(f32[96,768]{1,0:T(8,128)S(1)} %fusion.2, bf16[2,768,3072]{2,1,0:T(8,128)(2,1)} %param.10, bf16[1,96,3072]{2,1,0:T(8,128)(2,1)S(1)} %copy.103), kind=kOutput, calls=%fused_computation.13 | convolution fusion | flops 453058560 | bytes 5898240 | tf_op jit(solution)/shard_map/dot_general | solution.py:47
  70.2 3.9 %fusion.21 = f32[1,96,768]{2,1,0:T(8,128)S(1)} fusion(f32[96,768]{1,0:T(8,128)S(1)} %fusion, bf16[2,768,3072]{2,1,0:T(8,128)(2,1)} %param.10, bf16[1,96,3072]{2,1,0:T(8,128)(2,1)S(1)} %copy-done), kind=kOutput, calls=%fused_computation.15 | convolution fusion | flops 453058560 | bytes 5898240 | tf_op jit(solution)/shard_map/dot_general | solution.py:52
  74.2 1.2 copy.82
  75.4 0.1 fusion.64
  75.5 0.1 fusion.26
  75.7 0.1 fusion.68
  75.8 0.1 fusion.27
  76.0 147.0 %all-reduce.3.cloned.1.call-done = f32[2,96,768]{1,0,2:T(2,128)} async-done(((f32[2,96,768]{1,0,2:T(2,128)}), f32[2,96,768]{1,0,2:T(2,128)}) %all-reduce.3.cloned.1.call-update) | async-done | bytes 589840
  222.9 0.9 constant_dynamic-slice_fusion.1
  223.9 0.1 copy.89
  224.0 0.1 copy.84
  224.1 0.2 convolution_bitcast_fusion.2
  224.3 0.2 convolution_bitcast_fusion
  224.5 0.2 fusion.31
  224.7 0.2 fusion.33
  225.0 84.4 %psum.16 = f32[2,8,8]{2,1,0:T(8,128)S(1)} all-reduce(f32[2,8,8]{2,1,0:T(8,128)S(1)} %maximum_add_fusion), channel_id=1, replica_groups=mesh['bulk'=16,'wide'=16] {'bulk','wide'}, use_global_device_ids=true, to_apply=%region_1.2 | all-reduce | flops 128 | bytes 1024 | tf_op jit(solution)/shard_map/psum | solution.py:82
  309.5 0.6 maximum_add_fusion.2
  (34 shorter events, 1.6 us)
Async XLA Ops:
  6.5 42.8 %all-gather.2.cloned.1.call-start = ((), (), s32[]{:S(2)}) async-start(), calls=%async_computation | async-start | bytes 1671168 | tf_op jit(solution)/shard_map/all_gather | solution.py:46
  8.2 214.7 %all-reduce.3.cloned.1.call-start = ((), (), s32[]{:S(2)}) async-start(), calls=%async_computation.1 | async-start | bytes 1572864
  66.2 4.0 %copy-start = (bf16[1,96,3072]{2,1,0:T(8,128)(2,1)S(1)}, bf16[1,96,3072]{2,1,0:T(8,128)(2,1)}, u32[]{:S(2)}) copy-start(bf16[1,96,3072]{2,1,0:T(8,128)(2,1)} %copy.104) | copy-start | bytes 1769476
Sparse Core Ops, SparseCore 0:
  9.2 40.0 all-gather.1
  75.5 147.3 all-reduce.2
where the time goes:
time: 318 us; the launch traced here: 317 us
  waiting for transfers between devices  171 us (54%)
  blocking collectives  84.4 us (27%)
  matrix products  25 us (8%)
  local copies, waits for them, and re-layouts  16.8 us (5%)
  between operations  14.9 us (5%)
  other arithmetic  5.01 us (2%)
    unnamed x3, waiting for transfers between devices  147 us
    psum x1, blocking collectives, local(): lax.psum(main_part, ('bulk', 'wide'))  84.4 us
    all_gather x1, waiting for transfers between devices, local(): portion = lax.all_gather(weighted, 'bulk', axis=2, tiled=True)  23.8 us
  transfers between devices with their start and end apart: 2, of which 2 were waited for; matrix products, arithmetic and copies ran while one was open for 5% of the time, Pallas kernels for 0%

commit v1 on v0

v1 whole, which is shorter than its diff:
```python
import jax
import jax.numpy as jnp
from jax import lax
from jax.experimental import pallas as pl
from jax.experimental.pallas import tpu as pltpu
from jax.sharding import PartitionSpec as P

NT = 8
NL = 12
NVAL = 12
PAIRS = 96
ROWS = 768
COLS = 3072
UNITS = 8
UNIT = 384
OWN = 192
OWN_ROWS = 48
WIDE = 16
BULK = 16
HIGHEST = lax.Precision.HIGHEST
MESH = pl.DeviceIdType.MESH
OFFSETS = ((0, 0), (1, 0), (0, 1), (0, 3), (1, 1), (1, 3), (0, 2), (1, 2))
CONTRACT_LAST = (((1,), (1,)), ((), ()))


def dot(a, b, **kw):
    return jnp.dot(a, b, preferred_element_type=jnp.float32, **kw)


def dot_t(a, b, **kw):
    return lax.dot_general(a, b, CONTRACT_LAST, preferred_element_type=jnp.float32, **kw)


def iota(shape, dim):
    return lax.broadcasted_iota(jnp.int32, shape, dim)


def kernel(
    eps_hbm,
    rows_hbm,
    cols_hbm,
    coulomb_hbm,
    wing_row_hbm,
    wing_col_hbm,
    head_hbm,
    head_value_ref,
    head_coulomb_ref,
    bands_ref,
    out_ref,
    eps,
    rows,
    cols,
    coulomb,
    wing_row,
    wing_col,
    head,
    parcels,
    row_blocks,
    image,
    spread_hi,
    spread_lo,
    base,
    part_a,
    part_b,
    eps_sem,
    in_sem,
    parcel_send,
    parcel_recv,
    pass_send,
    row_send,
    row_recv,
    a_send,
    a_recv,
    b_send,
    b_recv,
):
    bulk = lax.axis_index("bulk")
    wide = lax.axis_index("wide")
    core = lax.rem(bulk, 2)
    chip = lax.div(bulk, 2)
    x_lo = lax.div(chip, 4)
    y = lax.rem(chip, 4)

    def unit_at(dx, dy):
        return lax.rem(x_lo + dx, 2) * 4 + lax.rem(y + dy, 4)

    units = [unit_at(dx, dy) for dx, dy in OFFSETS]

    small = [
        pltpu.make_async_copy(src, dst, in_sem.at[i])
        for i, (src, dst) in enumerate(
            (
                (cols_hbm, cols),
                (coulomb_hbm, coulomb),
                (rows_hbm, rows),
                (head_hbm, head),
                (wing_row_hbm, wing_row),
                (wing_col_hbm, wing_col),
            )
        )
    ]
    for copy in small:
        copy.start()
    slabs = []
    for i, unit in enumerate(units):
        span = pl.ds(pl.multiple_of(unit * UNIT, 128), UNIT)
        copy = pltpu.make_async_copy(eps_hbm.at[:, :, span], eps.at[:, :, span], eps_sem.at[i])
        copy.start()
        slabs.append(copy)

    barrier = pltpu.get_barrier_semaphore()
    for k in range(1, BULK):
        pl.semaphore_signal(
            barrier, inc=1, device_id={"bulk": lax.rem(bulk + k, BULK), "wide": wide}, device_id_type=MESH
        )
    for k in range(1, WIDE):
        pl.semaphore_signal(
            barrier, inc=1, device_id={"bulk": bulk, "wide": lax.rem(wide + k, WIDE)}, device_id_type=MESH
        )

    small[0].wait()
    small[1].wait()
    weighted = coulomb[...][None] * cols[...].astype(jnp.float32)
    weighted_pairs = weighted.reshape(2 * PAIRS, OWN)
    first = core == 0
    main = jnp.where(first, weighted_pairs[:, 0:128], weighted_pairs[:, 64:192])
    near = jnp.where(first, weighted[0][:, 128:192], weighted[1][:, 0:64])
    far = jnp.where(first, weighted[1][:, 128:192], weighted[0][:, 0:64])
    mine = parcels.at[chip, core]
    mine[0:192, :] = main.astype(jnp.bfloat16)
    mine[192:288, :] = jnp.concatenate([near, far], axis=1).astype(jnp.bfloat16)
    small[2].wait()
    wide_rows = rows[...].astype(jnp.float32)
    gap = jnp.zeros((PAIRS, 16), jnp.float32)
    row_blocks[wide] = jnp.concatenate([wide_rows[0], gap, wide_rows[1], gap], axis=1).astype(jnp.bfloat16)

    pl.semaphore_wait(barrier, BULK + WIDE - 2)

    sends = []

    def send(src, dst, send_sem, recv_sem, to_bulk, to_wide):
        copy = pltpu.make_async_remote_copy(
            src_ref=src,
            dst_ref=dst,
            send_sem=send_sem,
            recv_sem=recv_sem,
            device_id={"bulk": to_bulk, "wide": to_wide},
            device_id_type=MESH,
        )
        copy.start()
        sends.append(copy)

    sibling = chip * 2 + 1 - core
    send(mine, mine, pass_send.at[0], parcel_recv.at[chip, core], sibling, wide)
    for i, unit in enumerate(units[1:]):
        send(mine, mine, parcel_send.at[i], parcel_recv.at[chip, core], unit * 2 + core, wide)
    for k in (1, 15, 8, 2, 14, 9, 7, 3, 13, 10, 6, 4, 12, 11, 5):
        place = row_blocks.at[wide]
        send(place, place, row_send.at[k], row_recv.at[wide], bulk, lax.rem(wide + k, WIDE))

    for copy in small[3:]:
        copy.wait()
    pair_re = head[0:1, :]
    pair_im = head[1:2, :]
    head_row = jnp.concatenate([pair_re, pair_im], axis=1)
    turned_row = jnp.concatenate([-pair_im, pair_re], axis=1)
    both = 2 * PAIRS
    diagonal = iota((both, both), 0) == iota((both, both), 1)
    head_col = jnp.sum(jnp.where(diagonal, head_row, 0.0), axis=1, keepdims=True)
    coulomb_zero = head_coulomb_ref[0]
    scaled_row = coulomb_zero * head_row
    scaled_turned = coulomb_zero * turned_row
    weighted_low = weighted_pairs.astype(jnp.bfloat16)
    weighted_turned = jnp.concatenate([-weighted_low[PAIRS:], weighted_low[:PAIRS]], axis=0)
    wing_cols = wing_row[...]
    gain = dot_t(wing_cols, weighted_low)[0:1] + dot_t(wing_cols, weighted_turned)[1:2]
    rows_own = wide_rows.reshape(both, OWN_ROWS)
    wing_rows = wing_col[...].astype(jnp.float32)
    tilt_re = jnp.sum(rows_own * wing_rows[0:1], axis=1, keepdims=True)
    tilt_im = jnp.sum(rows_own * wing_rows[1:2], axis=1, keepdims=True)
    leads = jnp.where(jnp.logical_and(bulk == 0, wide == 0), 1.0, 0.0)
    from_head = gain + leads * (head_value_ref[0] * scaled_row + head_value_ref[1] * scaled_turned)
    base[...] = head_col * from_head + tilt_re * scaled_row + tilt_im * scaled_turned

    left_l = lax.rem(iota((both, both), 0), NL)
    right_l = lax.rem(iota((both, both), 1), NL)
    lane_l = lax.rem(iota((1, both), 1), NL)
    weight_row = jnp.zeros((1, both), jnp.float32)
    for l in range(NL):
        weight_row = jnp.where(lane_l == l, jnp.where(bands_ref[l] < NVAL, -0.5, 0.5), weight_row)
    mask = jnp.where(left_l == right_l, weight_row, 0.0)

    blank = jnp.zeros((16, both), jnp.bfloat16)
    for k in range(2 * WIDE):
        spread_hi[64 * k + 48 : 64 * k + 64, :] = blank
        spread_lo[64 * k + 48 : 64 * k + 64, :] = blank

    low_lanes = iota((PAIRS, 128), 1) < 64

    def halves(unit):
        head_block = parcels[unit, 0, 0:192, :]
        tail_block = parcels[unit, 1, 0:192, :]
        half0 = parcels[unit, 0, 192:288, :].astype(jnp.float32)
        half1 = parcels[unit, 1, 192:288, :].astype(jnp.float32)
        mid_re = jnp.where(low_lanes, half0, half1)
        mid_im = pltpu.roll(jnp.where(low_lanes, half1, half0), 64, 1)
        middle = jnp.concatenate([mid_re, mid_im], axis=0).astype(jnp.bfloat16)
        straight = jnp.concatenate([head_block, middle, tail_block], axis=1)
        turned = jnp.concatenate([-straight[PAIRS:], straight[:PAIRS]], axis=0)
        return jnp.concatenate([straight, turned], axis=1)

    def arrived(unit, of_core):
        place = parcels.at[unit, of_core]
        pltpu.make_async_copy(place, place, parcel_recv.at[unit, of_core]).wait()

    for i, unit in enumerate(units):
        if i + 1 < UNITS:
            later = units[i + 1]
            arrived(later, core)
            place = parcels.at[later, core]
            send(place, place, pass_send.at[i + 1], parcel_recv.at[later, core], sibling, wide)
        arrived(unit, 1 - core)
        slabs[i].wait()
        span = pl.ds(pl.multiple_of(unit * UNIT, 128), UNIT)
        slab = jnp.concatenate([eps[0, :, span], eps[1, :, span]], axis=1)
        term = dot_t(slab, halves(unit))
        if i == 0:
            image[...] = term
        else:
            image[...] += term

    for k in range(WIDE):
        block = image[OWN_ROWS * k : OWN_ROWS * (k + 1), :]
        high = block.astype(jnp.bfloat16)
        low = (block - high.astype(jnp.float32)).astype(jnp.bfloat16)
        for at in (128 * k, 128 * k + 64):
            spread_hi[at : at + OWN_ROWS, :] = high
            spread_lo[at : at + OWN_ROWS, :] = low

    for k in range(1, WIDE):
        place = row_blocks.at[lax.rem(wide + k, WIDE)]
        pltpu.make_async_copy(place, place, row_recv.at[lax.rem(wide + k, WIDE)]).wait()
    zero = jnp.zeros((PAIRS, 128), jnp.bfloat16)
    blocks = [row_blocks[k] for k in range(WIDE)]
    left = jnp.concatenate(
        [
            jnp.concatenate([jnp.where(low_lanes, b, zero) for b in blocks], axis=1),
            jnp.concatenate([jnp.where(low_lanes, zero, b) for b in blocks], axis=1),
        ],
        axis=0,
    )
    pairs = mask * (base[...] + dot(left, spread_hi[...]) + dot(left, spread_lo[...]))

    band = lax.div(iota((2 * NT, both), 1), NL)
    gather_rows = jnp.where(band == iota((2 * NT, both), 0), 1.0, 0.0)
    by_rows = dot(gather_rows, pairs, precision=HIGHEST)
    lane = iota((both, 128), 1)
    of_pair = lax.div(iota((both, 128), 0), NL)
    same = jnp.where(lane == of_pair, 1.0, 0.0)
    crossed = jnp.where(lane == of_pair - NT, 1.0, 0.0) - jnp.where(lane == of_pair + NT, 1.0, 0.0)
    crossed = jnp.where(lane < 2 * NT, crossed, 0.0)
    share = dot(by_rows[0:NT], same, precision=HIGHEST) + dot(by_rows[NT:], crossed, precision=HIGHEST)

    part_a[bulk] = share
    for k in range(1, BULK):
        place = part_a.at[bulk]
        send(place, place, a_send.at[k], a_recv.at[bulk], lax.rem(bulk + k, BULK), wide)
    for k in range(1, BULK):
        place = part_a.at[lax.rem(bulk + k, BULK)]
        pltpu.make_async_copy(place, place, a_recv.at[lax.rem(bulk + k, BULK)]).wait()
    part_b[wide] = jnp.sum(part_a[...], axis=0)
    for k in range(1, WIDE):
        place = part_b.at[wide]
        send(place, place, b_send.at[k], b_recv.at[wide], bulk, lax.rem(wide + k, WIDE))
    for k in range(1, WIDE):
        place = part_b.at[lax.rem(wide + k, WIDE)]
        pltpu.make_async_copy(place, place, b_recv.at[lax.rem(wide + k, WIDE)]).wait()
    total = jnp.sum(part_b[...], axis=0)
    out_ref[0] = total[:, 0:NT]
    out_ref[1] = total[:, NT : 2 * NT]
    for copy in sends:
        copy.wait_send()


def local(eps_corr, pair_rows, pair_cols, coulomb, wing_row, wing_col, pair_head, head_value, head_coulomb, inner_bands):
    bf16, f32 = jnp.bfloat16, jnp.float32
    dma = pltpu.SemaphoreType.DMA
    return pl.pallas_call(
        kernel,
        out_shape=jax.ShapeDtypeStruct((2, NT, NT), f32),
        in_specs=[pl.BlockSpec(memory_space=pl.ANY)] * 7 + [pl.BlockSpec(memory_space=pltpu.SMEM)] * 3,
        out_specs=pl.BlockSpec(memory_space=pltpu.VMEM),
        scratch_shapes=[
            pltpu.VMEM((2, ROWS, COLS), bf16),
            pltpu.VMEM((2, PAIRS, OWN_ROWS), bf16),
            pltpu.VMEM((2, PAIRS, OWN), bf16),
            pltpu.VMEM((1, OWN), f32),
            pltpu.VMEM((2, OWN), bf16),
            pltpu.VMEM((2, OWN_ROWS), bf16),
            pltpu.VMEM((2, PAIRS), f32),
            pltpu.VMEM((UNITS, 2, 288, 128), bf16),
            pltpu.VMEM((WIDE, PAIRS, 128), bf16),
            pltpu.VMEM((ROWS, 2 * PAIRS), f32),
            pltpu.VMEM((WIDE * 128, 2 * PAIRS), bf16),
            pltpu.VMEM((WIDE * 128, 2 * PAIRS), bf16),
            pltpu.VMEM((2 * PAIRS, 2 * PAIRS), f32),
            pltpu.VMEM((BULK, NT, 128), f32),
            pltpu.VMEM((WIDE, NT, 128), f32),
            dma((UNITS,)),
            dma((6,)),
            dma((UNITS - 1,)),
            dma((UNITS, 2)),
            dma((UNITS,)),
            dma((WIDE,)),
            dma((WIDE,)),
            dma((BULK,)),
            dma((BULK,)),
            dma((WIDE,)),
            dma((WIDE,)),
        ],
        compiler_params=pltpu.CompilerParams(
            collective_id=0, has_side_effects=True, vmem_limit_bytes=40 * 1024 * 1024
        ),
    )(
        eps_corr,
        pair_rows,
        pair_cols,
        coulomb.reshape(1, OWN),
        wing_row,
        wing_col,
        pair_head,
        head_value,
        head_coulomb,
        inner_bands,
    )


def solution(mesh):
    placed = (
        P(None, "bulk", "wide"),
        P(None, None, ("bulk", "wide")),
        P(None, None, ("wide", "bulk")),
        P(("wide", "bulk")),
        P(None, ("wide", "bulk")),
        P(None, ("bulk", "wide")),
        P(),
        P(),
        P(),
        P(),
    )
    return jax.shard_map(local, mesh=mesh, in_specs=placed, out_specs=P(), check_vma=False)
```

time: 318 us -> 52.6 us (0.17)
  waiting for transfers between devices: 171 us -> 0 us
  blocking collectives: 84.4 us -> 0 us
  Pallas kernels: 0 us -> 41.6 us
  matrix products: 25 us -> 0 us
  between operations: 14.9 us -> 0.68 us
  local copies, waits for them, and re-layouts: 16.8 us -> 10 us
  other arithmetic: 5.01 us -> 0 us
    unnamed x3 -> x0, waiting for transfers between devices: 147 us -> none
    psum x1 -> x0, blocking collectives: 84.4 us -> none  [local(): lax.psum(main_part, ('bulk', 'wide'))]
    pallas_call x0 -> x1, Pallas kernels: none -> 41.6 us  [local(): pl.pallas_call(kernel, out_shape=jax.ShapeDtypeStruct((2, NT, NT), f32),...]
    dot_general x28 -> x0, matrix products: 25 us -> none  [the longest x1 4.11 us: local(): lax.dot_general(portion[1], eps_corr[1], contract_last, preferred_element...]
    all_gather x1 -> x0, waiting for transfers between devices: 23.8 us -> none  [local(): portion = lax.all_gather(weighted, 'bulk', axis=2, tiled=True)]
    slice x5 -> x0, local copies, waits for them, and re-layouts: 7.47 us -> none  [the longest x1 4.39 us: local(): portion[1]]
    unnamed x5 -> x18, local copies, waits for them, and re-layouts: 5.73 us -> 10 us
  transfers between devices with their start and end apart: 2 -> 0, of which waited for: 2 -> 0; matrix products, arithmetic and copies ran while one was open for 5% -> 0% of each run, Pallas kernels for 0% -> 0%
where the time goes in v1:
time: 52.6 us; the launch traced here: 52.3 us
  Pallas kernels  41.6 us (79%)
  local copies, waits for them, and re-layouts  10 us (19%)
  between operations  0.68 us (1%)
    pallas_call x1, Pallas kernels, local(): pl.pallas_call(kernel, out_shape=jax.ShapeDtypeStruct((2, NT, NT), f32),...  41.6 us
    unnamed x18, local copies, waits for them, and re-layouts  10 us

profile of v1, /device:TPU:1, one launch (start us, length us, event | category | flops | bytes accessed | tf_op | source)
XLA Modules:
  0.0 52.3 jit_solution(460253143492539994)
XLA Ops:
  0.7 0.8 %copy.11.rows_hbm = bf16[2,96,48]{2,1,0:T(8,128)(2,1)S(1)} copy(bf16[2,96,48]{1,2,0:T(8,128)(2,1)} %param.11) | data formatting | bytes 36864 | tf_op args[1]
  1.5 0.0 copy-start
  1.5 3.7 %copy-done = bf16[2,768,3072]{2,1,0:T(8,128)(2,1)S(1)} copy-done((bf16[2,768,3072]{2,1,0:T(8,128)(2,1)S(1)}, bf16[2,768,3072]{2,1,0:T(8,128)(2,1)}, u32[]{:S(2)}) %copy-start) | copy-done | bytes 9437208
  5.2 0.0 copy-start.1
  5.2 0.9 %copy-done.1 = bf16[2,96,192]{2,1,0:T(8,128)(2,1)S(1)} copy-done((bf16[2,96,192]{2,1,0:T(8,128)(2,1)S(1)}, bf16[2,96,192]{2,1,0:T(8,128)(2,1)}, u32[]{:S(2)}) %copy-start.1) | copy-done | bytes 73752
  6.1 0.0 copy-start.2
  6.1 0.7 %copy-done.2 = f32[192]{0:T(256)S(1)} copy-done((f32[192]{0:T(256)S(1)}, f32[192]{0:T(256)}, u32[]{:S(2)}) %copy-start.2) | copy-done | bytes 792
  6.8 0.0 copy-start.3
  6.8 0.7 %copy-done.3 = bf16[2,192]{1,0:T(2,128)(2,1)S(1)} copy-done((bf16[2,192]{1,0:T(2,128)(2,1)S(1)}, bf16[2,192]{1,0:T(2,128)(2,1)}, u32[]{:S(2)}) %copy-start.3) | copy-done | bytes 792
  7.4 0.0 copy-start.4
  7.4 0.7 %copy-done.4 = f32[2,96]{1,0:T(2,128)S(1)} copy-done((f32[2,96]{1,0:T(2,128)S(1)}, f32[2,96]{1,0:T(2,128)}, u32[]{:S(2)}) %copy-start.4) | copy-done | bytes 792
  8.1 0.0 copy-start.5
  8.1 0.7 %copy-done.5 = bf16[2,48]{1,0:T(2,128)(2,1)S(1)} copy-done((bf16[2,48]{1,0:T(2,128)(2,1)S(1)}, bf16[2,48]{1,0:T(2,128)(2,1)}, u32[]{:S(2)}) %copy-start.5) | copy-done | bytes 216
  8.8 0.0 copy-start.6
  8.8 0.7 %copy-done.6 = f32[2]{0:T(128)S(1)} copy-done((f32[2]{0:T(128)S(1)}, f32[2]{0:T(128)}, u32[]{:S(2)}) %copy-start.6) | copy-done | bytes 32
  9.4 0.0 copy-start.7
  9.4 0.7 %copy-done.7 = s32[12]{0:T(128)S(1)} copy-done((s32[12]{0:T(128)S(1)}, s32[12]{0:T(128)}, u32[]{:S(2)}) %copy-start.7) | copy-done | bytes 72
  10.1 41.6 %shard_map.100 = f32[2,8,8]{2,1,0:T(8,128)S(1)} custom-call(bf16[2,768,3072]{2,1,0:T(8,128)(2,1)S(1)} %copy-done, bf16[2,96,48]{2,1,0:T(8,128)(2,1)S(1)} %copy.11.rows_hbm, bf16[2,96,192]{2,1,0:T(8,128)(2,1)S(1)} %copy-done.1, f32[1,192]{1,0:T(1,128)S(1)} %bitcast.1, bf16[2,192]{1,0:T(2,128)(2,1)S(1)} %copy-done.3, bf16[2,48]{1,0:T(2,128)(2,1)S(1)} %copy-done.5, ...), custom_call_target="tpu_custom_call" | custom-call | tf_op jit(solution)/shard_map/pallas_call | solution.py:288
  51.7 0.6 %copy.14 = f32[2,8,8]{2,1,0:T(8,128)} copy(f32[2,8,8]{2,1,0:T(8,128)S(1)} %shard_map.100) | data formatting | bytes 1024
Async XLA Ops:
  1.5 3.7 %copy-start = (bf16[2,768,3072]{2,1,0:T(8,128)(2,1)S(1)}, bf16[2,768,3072]{2,1,0:T(8,128)(2,1)}, u32[]{:S(2)}) copy-start(bf16[2,768,3072]{2,1,0:T(8,128)(2,1)} %eps_hbm.1) | copy-start | bytes 28311556
  5.2 0.9 %copy-start.1 = (bf16[2,96,192]{2,1,0:T(8,128)(2,1)S(1)}, bf16[2,96,192]{2,1,0:T(8,128)(2,1)}, u32[]{:S(2)}) copy-start(bf16[2,96,192]{2,1,0:T(8,128)(2,1)} %cols_hbm.1) | copy-start | bytes 221188
  6.1 0.7 %copy-start.2 = (f32[192]{0:T(256)S(1)}, f32[192]{0:T(256)}, u32[]{:S(2)}) copy-start(f32[192]{0:T(256)} %param.13) | copy-start | bytes 2308
  6.8 0.7 %copy-start.3 = (bf16[2,192]{1,0:T(2,128)(2,1)S(1)}, bf16[2,192]{1,0:T(2,128)(2,1)}, u32[]{:S(2)}) copy-start(bf16[2,192]{1,0:T(2,128)(2,1)} %wing_row_hbm.1) | copy-start | bytes 2308
  7.4 0.7 %copy-start.4 = (f32[2,96]{1,0:T(2,128)S(1)}, f32[2,96]{1,0:T(2,128)}, u32[]{:S(2)}) copy-start(f32[2,96]{1,0:T(2,128)} %head_hbm.1) | copy-start | bytes 2308
  8.1 0.7 %copy-start.5 = (bf16[2,48]{1,0:T(2,128)(2,1)S(1)}, bf16[2,48]{1,0:T(2,128)(2,1)}, u32[]{:S(2)}) copy-start(bf16[2,48]{1,0:T(2,128)(2,1)} %wing_col_hbm.1) | copy-start | bytes 580
  8.8 0.7 %copy-start.6 = (f32[2]{0:T(128)S(1)}, f32[2]{0:T(128)}, u32[]{:S(2)}) copy-start(f32[2]{0:T(128)} %head_value_ref.1) | copy-start | bytes 28
  9.4 0.7 %copy-start.7 = (s32[12]{0:T(128)S(1)}, s32[12]{0:T(128)}, u32[]{:S(2)}) copy-start(s32[12]{0:T(128)} %bands_ref.1) | copy-start | bytes 148

commit v2 on v1

v2 whole, which is shorter than its diff:
```python
import jax
import jax.numpy as jnp
from jax import lax
from jax.experimental import pallas as pl
from jax.experimental.pallas import tpu as pltpu
from jax.sharding import PartitionSpec as P

NT = 8
NL = 12
NVAL = 12
PAIRS = 96
BOTH = 192
ROWS = 768
COLS = 3072
UNITS = 8
UNIT = 384
OWN = 192
OWN_ROWS = 48
N_Z = 8
WIDE = 16
BULK = 16
BLOCK = 80
CUT = 48
STEPS = (0, 1, -1, 2, -2, 3, -3, 4)
HIGHEST = lax.Precision.HIGHEST
MESH = pl.DeviceIdType.MESH
CONTRACT_LAST = (((1,), (1,)), ((), ()))


def dot(a, b, **kw):
    return jnp.dot(a, b, preferred_element_type=jnp.float32, **kw)


def dot_t(a, b, **kw):
    return lax.dot_general(a, b, CONTRACT_LAST, preferred_element_type=jnp.float32, **kw)


def iota(shape, dim):
    return lax.broadcasted_iota(jnp.int32, shape, dim)


def split(value):
    high = value.astype(jnp.bfloat16)
    return high, (value - high.astype(jnp.float32)).astype(jnp.bfloat16)


def kernel(
    eps_hbm,
    rows_hbm,
    cols_hbm,
    coulomb_hbm,
    wing_row_hbm,
    wing_col_hbm,
    head_hbm,
    head_value_hbm,
    head_coulomb_hbm,
    bands_hbm,
    out_ref,
    eps,
    rows,
    cols,
    coulomb,
    wing_row,
    wing_col,
    head,
    head_value_ref,
    head_coulomb_ref,
    bands_ref,
    parcels,
    row_blocks,
    rows_stack,
    rows_turned,
    order,
    fold,
    image,
    image_high,
    image_low,
    base,
    part_a,
    part_b,
    eps_sem,
    in_sem,
    parcel_send,
    parcel_recv,
    row_send,
    row_recv,
    a_send,
    a_recv,
    b_send,
    b_recv,
):
    bulk = lax.axis_index("bulk")
    wide = lax.axis_index("wide")
    core = lax.rem(bulk, 2)
    chip = lax.div(bulk, 2)
    x_lo = lax.div(chip, 4)
    y = lax.rem(chip, 4)
    x_hi = lax.div(wide, N_Z)
    z = lax.rem(wide, N_Z)

    def unit_at(dx, dy):
        return lax.rem(x_lo + dx, 2) * 4 + lax.rem(y + dy, 4)

    def z_at(dz):
        return lax.rem(z + dz + N_Z, N_Z)

    here, across = unit_at(0, 0), unit_at(1, 0)
    along = [unit_at(0, 1), unit_at(0, 3), unit_at(0, 2)]
    aslant = [unit_at(1, 1), unit_at(1, 3), unit_at(1, 2)]
    units = [here, across] + along + aslant

    small = [
        pltpu.make_async_copy(src, dst, in_sem.at[i])
        for i, (src, dst) in enumerate(
            (
                (rows_hbm, rows),
                (cols_hbm, cols),
                (coulomb_hbm, coulomb),
                (head_hbm, head),
                (wing_row_hbm, wing_row),
                (wing_col_hbm, wing_col),
                (head_value_hbm, head_value_ref),
                (head_coulomb_hbm, head_coulomb_ref),
                (bands_hbm, bands_ref),
            )
        )
    ]
    for copy in small:
        copy.start()

    sibling = chip * 2 + 1 - core
    across_x = lax.rem(x_hi + 1, 2) * N_Z + z

    def along_z(dz):
        return x_hi * N_Z + z_at(dz)

    barrier = pltpu.get_barrier_semaphore()
    greeted = [(bulk, across_x), (sibling, wide)]
    greeted += [(unit * 2 + core, wide) for unit in [across] + along]
    greeted += [(bulk, along_z(dz)) for dz in (1, -1, 2, -2)]
    for to_bulk, to_wide in greeted:
        pl.semaphore_signal(barrier, inc=1, device_id={"bulk": to_bulk, "wide": to_wide}, device_id_type=MESH)

    slabs = []
    for i, unit in enumerate(units):
        span = pl.ds(pl.multiple_of(unit * UNIT, 128), UNIT)
        copy = pltpu.make_async_copy(eps_hbm.at[:, :, span], eps.at[:, :, span], eps_sem.at[i])
        copy.start()
        slabs.append(copy)

    small[0].wait()
    rows_f32 = rows[...].astype(jnp.float32)
    rows_own = jnp.concatenate([rows_f32[0], rows_f32[1]], axis=1)
    mine_rows = row_blocks.at[wide]
    mine_rows[0:48] = rows_own[:, :128].astype(jnp.bfloat16)
    packed = jnp.concatenate([rows_own[0:24, 128:], rows_own[24:48, 128:]], axis=1)
    mine_rows[48:80] = jnp.concatenate([packed, jnp.zeros((8, 128), jnp.float32)], axis=0).astype(jnp.bfloat16)
    small[1].wait()
    small[2].wait()
    weighted = coulomb[...][None] * cols[...].astype(jnp.float32)
    weighted_pairs = weighted.reshape(BOTH, OWN)
    first = core == 0
    main = jnp.where(first, weighted_pairs[:, 0:128], weighted_pairs[:, 64:192])
    near = jnp.where(first, weighted[0][:, 128:192], weighted[1][:, 0:64])
    far = jnp.where(first, weighted[1][:, 128:192], weighted[0][:, 0:64])
    mine = parcels.at[bulk]
    mine[0:192, :] = main.astype(jnp.bfloat16)
    mine[192:288, :] = jnp.concatenate([near, far], axis=1).astype(jnp.bfloat16)

    pl.semaphore_wait(barrier, len(greeted))

    def send(place, send_sem, recv_sem, to_bulk, to_wide):
        pltpu.make_async_remote_copy(
            src_ref=place,
            dst_ref=place,
            send_sem=send_sem,
            recv_sem=recv_sem,
            device_id={"bulk": to_bulk, "wide": to_wide},
            device_id_type=MESH,
        ).start()

    def landed(place, sem):
        pltpu.make_async_copy(place, place, sem).wait()

    def send_parcel(of_bulk, to_bulk):
        send(parcels.at[of_bulk], parcel_send, parcel_recv.at[of_bulk], to_bulk, wide)

    def arrived(unit, of_core):
        at = unit * 2 + of_core
        landed(parcels.at[at], parcel_recv.at[at])

    def hand_on(unit):
        send_parcel(unit * 2 + core, sibling)

    def relay(unit, to_chip):
        send_parcel(unit * 2 + core, to_chip * 2 + core)

    def send_rows(of_wide, to_wide):
        send(row_blocks.at[of_wide], row_send, row_recv.at[of_wide, 0], bulk, to_wide)

    def rows_landed(of_wide):
        landed(row_blocks.at[of_wide], row_recv.at[of_wide, 0])

    send_rows(wide, across_x)
    relay(here, across)
    for dz in (2, -2, 1, -1):
        send_rows(wide, along_z(dz))
    for unit in along:
        relay(here, unit)
    hand_on(here)

    low_lanes = iota((PAIRS, 128), 1) < 64

    rows_landed(across_x)
    for dz in (2, -2, 1, -1):
        send_rows(across_x, along_z(dz))

    @pl.when(core == 0)
    def _():
        arrived(across, core)
        for unit in (along[2], along[0], along[1]):
            relay(across, unit)

    @pl.when(core == 1)
    def _():
        for unit in along[:2]:
            arrived(unit, core)
            relay(unit, across)
        arrived(across, core)

    hand_on(across)

    for copy in small[3:]:
        copy.wait()
    pair_re = head[0:1, :]
    pair_im = head[1:2, :]
    head_row = jnp.concatenate([pair_re, pair_im], axis=1)
    turned_row = jnp.concatenate([-pair_im, pair_re], axis=1)
    square = (BOTH, BOTH)
    row_at, lane_at = iota(square, 0), iota(square, 1)
    head_col = jnp.sum(jnp.where(row_at == lane_at, head_row, 0.0), axis=1, keepdims=True)
    coulomb_zero = head_coulomb_ref[0]
    scaled_row = coulomb_zero * head_row
    scaled_turned = coulomb_zero * turned_row
    weighted_low = (coulomb[...][None] * cols[...].astype(jnp.float32)).astype(jnp.bfloat16).reshape(BOTH, OWN)
    weighted_turned = jnp.concatenate([-weighted_low[PAIRS:], weighted_low[:PAIRS]], axis=0)
    wing_cols = wing_row[...]
    gain = dot_t(wing_cols, weighted_low)[0:1] + dot_t(wing_cols, weighted_turned)[1:2]
    rows_here = jnp.swapaxes(rows[...].astype(jnp.float32), 1, 2).reshape(BOTH, OWN_ROWS)
    wing_rows = wing_col[...].astype(jnp.float32)
    tilt_re = jnp.sum(rows_here * wing_rows[0:1], axis=1, keepdims=True)
    tilt_im = jnp.sum(rows_here * wing_rows[1:2], axis=1, keepdims=True)
    leads = jnp.where(jnp.logical_and(bulk == 0, wide == 0), 1.0, 0.0)
    from_head = gain + leads * (head_value_ref[0] * scaled_row + head_value_ref[1] * scaled_turned)
    outer = head_col * from_head + tilt_re * scaled_row + tilt_im * scaled_turned
    lane_l = lax.rem(iota((1, BOTH), 1), NL)
    weight_row = jnp.zeros((1, BOTH), jnp.float32)
    for l in range(NL):
        weight_row = jnp.where(lane_l == l, jnp.where(bands_ref[l] < NVAL, -0.5, 0.5), weight_row)
    outer = jnp.where(lax.rem(row_at, NL) == lax.rem(lane_at, NL), weight_row * outer, 0.0)

    pick = (BOTH, 128)
    from_q, to_lane = iota(pick, 0), iota(pick, 1)
    same_band = lax.div(lax.rem(from_q, PAIRS), NL) == lax.rem(to_lane, NT)
    part_q, part_lane = lax.div(from_q, PAIRS), lax.div(to_lane, 64)
    straight = jnp.where(jnp.logical_and(same_band, part_q == part_lane), 1.0, 0.0)
    sign = jnp.where(part_lane == 0, 1.0, -1.0)
    crossed = jnp.where(jnp.logical_and(same_band, part_q != part_lane), sign, 0.0)
    fold[0] = straight.astype(jnp.bfloat16)
    fold[1] = crossed.astype(jnp.bfloat16)
    band_lanes = lax.rem(lax.div(iota((NT, 128), 1), NT), NT) == iota((NT, 128), 0)
    band = lax.div(iota((2 * NT, BOTH), 1), NL)
    gather_rows = jnp.where(band == iota((2 * NT, BOTH), 0), 1.0, 0.0)
    by_rows = dot(gather_rows, outer, precision=HIGHEST)
    base[...] = dot(by_rows[0:NT], straight, precision=HIGHEST) + dot(by_rows[NT:], crossed, precision=HIGHEST)
    same_l = lax.rem(lane_at, NL) == lax.div(lax.rem(row_at, PAIRS), NT)
    same_n = lax.div(lax.rem(lane_at, PAIRS), NL) == lax.rem(row_at, NT)
    same_part = lax.div(lane_at, PAIRS) == lax.div(row_at, PAIRS)
    chosen = jnp.logical_and(jnp.logical_and(same_l, same_n), same_part)
    order[...] = jnp.where(chosen, weight_row, 0.0).astype(jnp.bfloat16)

    def work(i):
        unit = units[i]
        arrived(unit, 1 - core)
        slabs[i].wait()
        head_block = parcels[unit * 2, 0:192, :]
        tail_block = parcels[unit * 2 + 1, 0:192, :]
        half0 = parcels[unit * 2, 192:288, :]
        half1 = parcels[unit * 2 + 1, 192:288, :]
        mid_re = jnp.where(low_lanes, half0, half1)
        mid_im = jnp.where(low_lanes, half1, half0)
        mid_im = jnp.concatenate([mid_im[:, 64:], mid_im[:, :64]], axis=1)
        middle = jnp.concatenate([mid_re, mid_im], axis=0)
        plain = jnp.concatenate([head_block, middle, tail_block], axis=1)
        turned = jnp.concatenate([-plain[PAIRS:], plain[:PAIRS]], axis=0)
        span = pl.ds(pl.multiple_of(unit * UNIT, 128), UNIT)
        slab = jnp.concatenate([eps[0, :, span], eps[1, :, span]], axis=1)
        term = dot_t(slab, jnp.concatenate([plain, turned], axis=1))
        if i == 0:
            image[...] = term
        else:
            image[...] += term

    work(0)

    for at_x in (x_hi, lax.rem(x_hi + 1, 2)):
        for i, dz in enumerate((1, -1)):
            source = at_x * N_Z + z_at(-2 * dz)
            rows_landed(source)
            piece = row_blocks.at[source, pl.ds(0, CUT) if dz == 1 else pl.ds(CUT, BLOCK - CUT)]
            send(piece, row_send, row_recv.at[source, i], bulk, along_z(2 * dz))
            send_rows(source, along_z(dz))

    @pl.when(core == 0)
    def _():
        for unit in along:
            arrived(unit, core)

    @pl.when(core == 1)
    def _():
        arrived(along[2], core)
        relay(along[2], across)

    for unit in along:
        hand_on(unit)

    for i in (1, 2, 3, 4):
        work(i)

    for unit in aslant:
        arrived(unit, core)
        hand_on(unit)

    def turn_rows(batch):
        for j in range(4 * batch, 4 * batch + 4):
            for half in range(2):
                source = half * N_Z + z_at(STEPS[j])
                at = 96 * j + 48 * half
                packed = row_blocks[source, 48:72, :].astype(jnp.float32)
                rest = jnp.concatenate([packed, pltpu.roll(packed, 64, 1)], axis=0)
                rows_stack[at : at + 48, 0:128] = row_blocks[source, 0:48, :]
                rows_stack[at : at + 48, 128:256] = rest.astype(jnp.bfloat16)
        span = slice(384 * batch, 384 * batch + 384)
        rows_turned[:, span] = dot_t(order[...], rows_stack[span, 0:BOTH]).astype(jnp.bfloat16)

    for dz in (1, -1):
        for half in range(2):
            rows_landed(half * N_Z + z_at(dz))
    turn_rows(0)

    for i in (5, 6, 7):
        work(i)

    def split_image(batch):
        for j in range(4 * batch, 4 * batch + 4):
            for half in range(2):
                source = half * N_Z + z_at(STEPS[j])
                at = 96 * j + 48 * half
                block = image[pl.ds(pl.multiple_of(source * OWN_ROWS, 16), OWN_ROWS), :]
                image_high[at : at + 48, :], image_low[at : at + 48, :] = split(block)

    def multiply(batch):
        span = slice(384 * batch, 384 * batch + 384)
        left = rows_turned[:, span]
        return dot(left, image_high[span, :]) + dot(left, image_low[span, :])

    split_image(0)
    split_image(1)
    for half in range(2):
        for dz in (3, -3):
            rows_landed(half * N_Z + z_at(dz))
        source = half * N_Z + z_at(4)
        landed(row_blocks.at[source, pl.ds(0, CUT)], row_recv.at[source, 0])
        landed(row_blocks.at[source, pl.ds(CUT, BLOCK - CUT)], row_recv.at[source, 1])
    turn_rows(1)
    pairs = multiply(0) + multiply(1)
    total = base[...]
    for half in range(2):
        kept = jnp.zeros((NT, BOTH), jnp.float32)
        for l in range(NL):
            at = PAIRS * half + NT * l
            kept = jnp.where(lane_l == l, pairs[at : at + NT, :], kept)
        high, low = split(kept)
        total = total + dot(high, fold[half]) + dot(low, fold[half])
    share = jnp.sum(jnp.where(band_lanes, total, 0.0), axis=0, keepdims=True)

    part_a[bulk] = share
    for k in (7, 15, 5, 13, 6, 14, 1, 3, 9, 11, 2, 4, 8, 10, 12):
        send(part_a.at[bulk], a_send, a_recv, lax.rem(bulk + k, BULK), wide)
    landed(parcels.at[pl.ds(0, 15)], parcel_send)
    landed(row_blocks.at[pl.ds(0, 15)], row_send)
    landed(part_a.at[pl.ds(0, BULK - 1)], a_recv)
    part_b[wide] = jnp.sum(part_a[...], axis=0)
    for k in (12, 4, 11, 13, 3, 5, 10, 14, 2, 6, 9, 15, 1, 7, 8):
        send(part_b.at[wide], b_send, b_recv, bulk, lax.rem(wide + k, WIDE))
    landed(part_a.at[pl.ds(0, BULK - 1)], a_send)
    landed(part_b.at[pl.ds(0, WIDE - 1)], b_recv)
    result = jnp.where(band_lanes, jnp.sum(part_b[...], axis=0), 0.0)
    lanes = iota((NT, 128), 1)
    for part in range(2):
        value = jnp.where(lax.div(lanes, 64) == part, result, 0.0)
        for shift in (8, 16, 32, 64):
            value = value + pltpu.roll(value, shift, 1)
        out_ref[part] = value[:, 0:NT]
    landed(part_b.at[pl.ds(0, WIDE - 1)], b_send)


def local(eps_corr, pair_rows, pair_cols, coulomb, wing_row, wing_col, pair_head, head_value, head_coulomb, inner_bands):
    bf16, f32 = jnp.bfloat16, jnp.float32
    dma = pltpu.SemaphoreType.DMA
    return pl.pallas_call(
        kernel,
        out_shape=jax.ShapeDtypeStruct((2, NT, NT), f32),
        in_specs=[pl.BlockSpec(memory_space=pltpu.HBM)] * 10,
        out_specs=pl.BlockSpec(memory_space=pltpu.VMEM),
        scratch_shapes=[
            pltpu.VMEM((2, ROWS, COLS), bf16),
            pltpu.VMEM((2, OWN_ROWS, PAIRS), bf16),
            pltpu.VMEM((2, PAIRS, OWN), bf16),
            pltpu.VMEM((1, OWN), f32),
            pltpu.VMEM((2, OWN), bf16),
            pltpu.VMEM((2, OWN_ROWS), bf16),
            pltpu.VMEM((2, PAIRS), f32),
            pltpu.SMEM((2,), f32),
            pltpu.SMEM((1,), f32),
            pltpu.SMEM((NL,), jnp.int32),
            pltpu.VMEM((BULK, 288, 128), bf16),
            pltpu.VMEM((WIDE, BLOCK, 128), bf16),
            pltpu.VMEM((ROWS, 256), bf16),
            pltpu.VMEM((BOTH, ROWS), bf16),
            pltpu.VMEM((BOTH, BOTH), bf16),
            pltpu.VMEM((2, BOTH, 128), bf16),
            pltpu.VMEM((ROWS, BOTH), f32),
            pltpu.VMEM((ROWS, BOTH), bf16),
            pltpu.VMEM((ROWS, BOTH), bf16),
            pltpu.VMEM((NT, 128), f32),
            pltpu.VMEM((16, 1, 128), f32),
            pltpu.VMEM((16, 1, 128), f32),
            dma((UNITS,)),
            dma((9,)),
            dma,
            dma((BULK,)),
            dma,
            dma((WIDE, 2)),
            dma,
            dma,
            dma,
            dma,
        ],
        compiler_params=pltpu.CompilerParams(
            collective_id=0, has_side_effects=True, vmem_limit_bytes=63 * 1024 * 1024
        ),
    )(
        eps_corr,
        jnp.swapaxes(pair_rows, 1, 2),
        pair_cols,
        coulomb.reshape(1, OWN),
        wing_row,
        wing_col,
        pair_head,
        head_value,
        head_coulomb,
        inner_bands,
    )


def solution(mesh):
    placed = (
        P(None, "bulk", "wide"),
        P(None, None, ("bulk", "wide")),
        P(None, None, ("wide", "bulk")),
        P(("wide", "bulk")),
        P(None, ("wide", "bulk")),
        P(None, ("bulk", "wide")),
        P(),
        P(),
        P(),
        P(),
    )
    return jax.shard_map(local, mesh=mesh, in_specs=placed, out_specs=P(), check_vma=False)
```

time: 52.6 us -> 37.5 us (0.71)
  local copies, waits for them, and re-layouts: 10 us -> 1.3 us
  Pallas kernels: 41.6 us -> 35.4 us
    unnamed x18 -> x1, local copies, waits for them, and re-layouts: 10 us -> 1.3 us
    pallas_call x1, Pallas kernels: 41.6 us -> 35.4 us  [local(): pl.pallas_call(kernel, out_shape=jax.ShapeDtypeStruct((2, NT, NT), f32),...]
where the time goes in v2:
time: 37.5 us; the launch traced here: 37.4 us
  Pallas kernels  35.4 us (94%)
  local copies, waits for them, and re-layouts  1.3 us (3%)
  between operations  0.66 us (2%)
    pallas_call x1, Pallas kernels, local(): pl.pallas_call(kernel, out_shape=jax.ShapeDtypeStruct((2, NT, NT), f32),...  35.4 us
    unnamed x1, local copies, waits for them, and re-layouts  1.3 us

profile of v2, /device:TPU:1, one launch (start us, length us, event | category | flops | bytes accessed | tf_op | source)
XLA Modules:
  0.0 37.4 jit_solution(2797964775436103873)
XLA Ops:
  0.7 35.4 %shard_map.100 = f32[2,8,8]{2,1,0:T(8,128)} custom-call(bf16[2,768,3072]{2,1,0:T(8,128)(2,1)} %eps_hbm.1, bf16[2,48,96]{2,1,0:T(8,128)(2,1)} %bitcast.2, bf16[2,96,192]{2,1,0:T(8,128)(2,1)} %cols_hbm.1, f32[1,192]{1,0:T(1,128)} %bitcast.3, bf16[2,192]{1,0:T(2,128)(2,1)} %wing_row_hbm.1, bf16[2,48]{1,0:T(2,128)(2,1)} %wing_col_hbm.1, f32[2,96]{1,0:T(2,128)} %head_hbm.1, ...), custom_call_target="tpu_custom_call" | custom-call | tf_op jit(solution)/shard_map/pallas_call | solution.py:411
  36.1 1.3 %copy.13 = f32[2,8,8]{2,1,0:T(8,128)} copy(f32[2,8,8]{2,1,0:T(8,128)} %shard_map.100) | data formatting | bytes 1024

commit v3 on v2

v3 whole, which is shorter than its diff:
```python
import jax
import jax.numpy as jnp
from jax import lax
from jax.experimental import pallas as pl
from jax.experimental.pallas import tpu as pltpu
from jax.sharding import PartitionSpec as P

NT = 8
NL = 12
NVAL = 12
PAIRS = 96
BOTH = 192
ROWS = 768
COLS = 3072
UNITS = 8
UNIT = 384
OWN = 192
OWN_ROWS = 48
N_Z = 8
WIDE = 16
BULK = 16
BLOCK = 80
CUT = 48
STEPS = (0, 1, -1, 2, -2, 3, -3, 4)
HIGHEST = lax.Precision.HIGHEST
MESH = pl.DeviceIdType.MESH
CONTRACT_LAST = (((1,), (1,)), ((), ()))


def dot(a, b, **kw):
    return jnp.dot(a, b, preferred_element_type=jnp.float32, **kw)


def dot_t(a, b, **kw):
    return lax.dot_general(a, b, CONTRACT_LAST, preferred_element_type=jnp.float32, **kw)


def iota(shape, dim):
    return lax.broadcasted_iota(jnp.int32, shape, dim)


def split(value):
    high = value.astype(jnp.bfloat16)
    return high, (value - high.astype(jnp.float32)).astype(jnp.bfloat16)


def kernel(
    eps_hbm,
    rows_hbm,
    cols_hbm,
    coulomb_hbm,
    wing_row_hbm,
    wing_col_hbm,
    head_hbm,
    head_value_hbm,
    head_coulomb_hbm,
    bands_hbm,
    out_ref,
    eps,
    rows,
    cols,
    coulomb,
    wing_row,
    wing_col,
    head,
    head_value_ref,
    head_coulomb_ref,
    bands_ref,
    parcels,
    own_weighted,
    row_blocks,
    rows_stack,
    rows_turned,
    order,
    fold,
    image,
    image_high,
    image_low,
    base,
    part_a,
    part_b,
    eps_sem,
    in_sem,
    parcel_send,
    parcel_recv,
    row_send,
    row_recv,
    a_send,
    a_recv,
    b_send,
    b_recv,
):
    bulk = lax.axis_index("bulk")
    wide = lax.axis_index("wide")
    core = lax.rem(bulk, 2)
    chip = lax.div(bulk, 2)
    x_lo = lax.div(chip, 4)
    y = lax.rem(chip, 4)
    x_hi = lax.div(wide, N_Z)
    z = lax.rem(wide, N_Z)

    def unit_at(dx, dy):
        return lax.rem(x_lo + dx, 2) * 4 + lax.rem(y + dy, 4)

    def unit_of(i):
        return unit_at(lax.div(i, 4), lax.rem(i, 4))

    def z_at(dz):
        return lax.rem(z + dz + N_Z, N_Z)

    here, across = unit_at(0, 0), unit_at(1, 0)

    def repeat(first, last, step):
        def body(i, carry):
            step(i)
            return carry

        lax.fori_loop(first, last, body, 0)

    small = [
        pltpu.make_async_copy(src, dst, in_sem.at[i])
        for i, (src, dst) in enumerate(
            (
                (rows_hbm, rows),
                (cols_hbm, cols),
                (coulomb_hbm, coulomb),
                (head_hbm, head),
                (wing_row_hbm, wing_row),
                (wing_col_hbm, wing_col),
                (head_value_hbm, head_value_ref),
                (head_coulomb_hbm, head_coulomb_ref),
                (bands_hbm, bands_ref),
            )
        )
    ]
    for copy in small:
        copy.start()

    sibling = chip * 2 + 1 - core
    across_x = lax.rem(x_hi + 1, 2) * N_Z + z

    def along_z(dz):
        return x_hi * N_Z + z_at(dz)

    barrier = pltpu.get_barrier_semaphore()

    def greet(to_bulk, to_wide):
        pl.semaphore_signal(barrier, inc=1, device_id={"bulk": to_bulk, "wide": to_wide}, device_id_type=MESH)

    greet(bulk, across_x)
    greet(sibling, wide)
    greet(across * 2 + core, wide)
    for dy in (1, 3, 2):
        greet(unit_at(0, dy) * 2 + core, wide)
    for dz in (1, -1, 2, -2):
        greet(bulk, along_z(dz))

    def slab(i):
        span = pl.ds(pl.multiple_of(unit_of(i) * UNIT, 128), UNIT)
        return pltpu.make_async_copy(eps_hbm.at[:, :, span], eps.at[i], eps_sem.at[i])

    repeat(0, UNITS, lambda i: slab(i).start())

    pl.semaphore_wait(barrier, 10)

    def send(place, send_sem, recv_sem, to_bulk, to_wide):
        pltpu.make_async_remote_copy(
            src_ref=place,
            dst_ref=place,
            send_sem=send_sem,
            recv_sem=recv_sem,
            device_id={"bulk": to_bulk, "wide": to_wide},
            device_id_type=MESH,
        ).start()

    def landed(place, sem):
        pltpu.make_async_copy(place, place, sem).wait()

    def send_parcel(of_bulk, to_bulk):
        send(parcels.at[of_bulk], parcel_send, parcel_recv.at[of_bulk], to_bulk, wide)

    def arrived(unit, of_core):
        at = unit * 2 + of_core
        landed(parcels.at[at], parcel_recv.at[at])

    def hand_on(unit):
        send_parcel(unit * 2 + core, sibling)

    def relay(unit, to_chip):
        send_parcel(unit * 2 + core, to_chip * 2 + core)

    def send_rows(of_wide, to_wide):
        send(row_blocks.at[of_wide], row_send, row_recv.at[of_wide, 0], bulk, to_wide)

    def rows_landed(of_wide):
        landed(row_blocks.at[of_wide], row_recv.at[of_wide, 0])

    small[0].wait()
    rows_f32 = rows[...].astype(jnp.float32)
    rows_own = jnp.concatenate([rows_f32[0], rows_f32[1]], axis=1)
    mine_rows = row_blocks.at[wide]
    rows_low = rows_own.astype(jnp.bfloat16)
    mine_rows[0:48] = rows_low[:, :128]
    packed = jnp.concatenate([rows_own[0:24, 128:], rows_own[24:48, 128:]], axis=1)
    mine_rows[48:80] = jnp.concatenate([packed, jnp.zeros((8, 128), jnp.float32)], axis=0).astype(jnp.bfloat16)
    send_rows(wide, across_x)
    small[1].wait()
    small[2].wait()
    weighted = coulomb[...][None] * cols[...].astype(jnp.float32)
    weighted_pairs = weighted.reshape(BOTH, OWN)
    first = core == 0
    main = jnp.where(first, weighted_pairs[:, 0:128], weighted_pairs[:, 64:192])
    near = jnp.where(first, weighted[0][:, 128:192], weighted[1][:, 0:64])
    far = jnp.where(first, weighted[1][:, 128:192], weighted[0][:, 0:64])
    mine = parcels.at[bulk]
    mine[0:192, :] = main.astype(jnp.bfloat16)
    own_weighted[...] = weighted_pairs.astype(jnp.bfloat16)
    mine[192:288, :] = jnp.concatenate([near, far], axis=1).astype(jnp.bfloat16)


    relay(here, across)

    def send_along(of_wide):
        def step(i):
            send_rows(of_wide, along_z(jnp.where(i < 2, i - 2, i - 1)))

        repeat(0, 4, step)

    send_along(wide)
    repeat(1, 4, lambda dy: relay(here, unit_at(0, dy)))
    hand_on(here)

    low_lanes = iota((PAIRS, 128), 1) < 64

    for copy in small[3:]:
        copy.wait()
    pair_re = head[0:1, :]
    pair_im = head[1:2, :]
    head_row = jnp.concatenate([pair_re, pair_im], axis=1)
    turned_row = jnp.concatenate([-pair_im, pair_re], axis=1)
    coulomb_zero = head_coulomb_ref[0]
    scaled_row = coulomb_zero * head_row
    scaled_turned = coulomb_zero * turned_row
    weighted_low = own_weighted[...]
    weighted_turned = jnp.concatenate([-weighted_low[PAIRS:], weighted_low[:PAIRS]], axis=0)
    wing_cols = wing_row[...]
    gain = dot_t(wing_cols, weighted_low)[0:1] + dot_t(wing_cols, weighted_turned)[1:2]
    tilt = dot(wing_col[...], rows_low)
    leads = jnp.where(jnp.logical_and(bulk == 0, wide == 0), 1.0, 0.0)
    from_head = gain + leads * (head_value_ref[0] * scaled_row + head_value_ref[1] * scaled_turned)
    lane = iota((1, BOTH), 1)
    lane_l = lax.rem(lane, NL)
    lane_band = lax.div(lane, NL)
    weight_row = jnp.zeros((1, BOTH), jnp.float32)
    for l in range(NL):
        weight_row = jnp.where(lane_l == l, jnp.where(bands_ref[l] < NVAL, -0.5, 0.5), weight_row)
    row_at = iota((BOTH, 1), 0)
    same_l = jnp.where(lax.rem(row_at, NL) == lane_l, weight_row, 0.0).astype(jnp.bfloat16)
    in_band = iota((2 * NT, BOTH), 0) == lane_band

    def gathered(row):
        spread = jnp.where(in_band, row, 0.0)
        high = spread.astype(jnp.bfloat16)
        middle, low = split(spread - high.astype(jnp.float32))
        return dot(high, same_l) + dot(middle, same_l) + dot(low, same_l)

    base[...] = (
        gathered(head_row) * from_head + gathered(tilt[0:1]) * scaled_row + gathered(tilt[1:2]) * scaled_turned
    )

    to_lane = iota((1, 128), 1)
    low_part = to_lane < 64
    key = jnp.where(low_part, 0, NT) + lax.rem(to_lane, NT)
    row_band = lax.div(row_at, NL)
    fold[0] = jnp.where(row_band == key, 1.0, 0.0).astype(jnp.bfloat16)
    sign = jnp.where(low_part, 1.0, -1.0)
    fold[1] = jnp.where(row_band == jnp.where(low_part, key + NT, key - NT), sign, 0.0).astype(jnp.bfloat16)
    band_lanes = lax.rem(lax.div(to_lane, NT), NT) == iota((NT, 128), 0)
    lane_half = lax.div(lane, PAIRS)
    place = lane_half * PAIRS + lane_l * NT + lane_band - lane_half * NT
    order[...] = jnp.where(iota((BOTH, BOTH), 0) == place, weight_row, 0.0).astype(jnp.bfloat16)
    image[...] = jnp.zeros((ROWS, BOTH), jnp.float32)

    rows_landed(across_x)
    send_along(across_x)

    @pl.when(core == 0)
    def _():
        arrived(across, core)
        repeat(1, 4, lambda dy: relay(across, unit_at(0, dy)))

    @pl.when(core == 1)
    def _():
        for dy in (1, 3):
            arrived(unit_at(0, dy), core)
            relay(unit_at(0, dy), across)
        arrived(across, core)

    hand_on(across)

    def work(i):
        unit = unit_of(i)
        arrived(unit, 1 - core)
        slab(i).wait()
        head_block = parcels[unit * 2, 0:192, :]
        tail_block = parcels[unit * 2 + 1, 0:192, :]
        half0 = parcels[unit * 2, 192:288, :]
        half1 = parcels[unit * 2 + 1, 192:288, :]
        mid_re = jnp.where(low_lanes, half0, half1)
        mid_im = jnp.where(low_lanes, half1, half0)
        mid_im = jnp.concatenate([mid_im[:, 64:], mid_im[:, :64]], axis=1)
        middle = jnp.concatenate([mid_re, mid_im], axis=0)
        plain = jnp.concatenate([head_block, middle, tail_block], axis=1)
        turned = jnp.concatenate([-plain[PAIRS:], plain[:PAIRS]], axis=0)
        left = jnp.concatenate([eps[i, 0], eps[i, 1]], axis=1)
        image[...] += dot_t(left, jnp.concatenate([plain, turned], axis=1))

    def relay_rows(at_x):
        for i, dz in enumerate((1, -1)):
            source = at_x * N_Z + z_at(-2 * dz)
            rows_landed(source)
            piece = row_blocks.at[source, pl.ds(0, CUT) if dz == 1 else pl.ds(CUT, BLOCK - CUT)]
            send(piece, row_send, row_recv.at[source, i], bulk, along_z(2 * dz))
            send_rows(source, along_z(dz))

    def second_stage():
        @pl.when(core == 0)
        def _():
            for dy in (1, 2, 3):
                arrived(unit_at(0, dy), core)

        @pl.when(core == 1)
        def _():
            arrived(unit_at(0, 2), core)
            relay(unit_at(0, 2), across)

        relay_rows(x_hi)
        repeat(1, 4, lambda dy: hand_on(unit_at(0, dy)))
        relay_rows(lax.rem(x_hi + 1, 2))

    def third_stage():
        def step(dy):
            arrived(unit_at(1, dy), core)
            hand_on(unit_at(1, dy))

        repeat(1, 4, step)

    def turn_rows(batch):
        for j in range(4 * batch, 4 * batch + 4):
            for half in range(2):
                source = half * N_Z + z_at(STEPS[j])
                at = 96 * j + 48 * half
                packed = row_blocks[source, 48:72, :].astype(jnp.float32)
                rest = jnp.concatenate([packed, pltpu.roll(packed, 64, 1)], axis=0)
                rows_stack[at : at + 48, 0:128] = row_blocks[source, 0:48, :]
                rows_stack[at : at + 48, 128:256] = rest.astype(jnp.bfloat16)
        span = slice(384 * batch, 384 * batch + 384)
        rows_turned[:, span] = dot_t(order[...], rows_stack[span, 0:BOTH]).astype(jnp.bfloat16)

    def units_step(i):
        @pl.when(i == 1)
        def _():
            second_stage()

        @pl.when(i == 5)
        def _():
            third_stage()

        work(i)

    repeat(0, UNITS, units_step)

    for dz in (1, -1):
        for half in range(2):
            rows_landed(half * N_Z + z_at(dz))
    turn_rows(0)

    def split_image(batch):
        for j in range(4 * batch, 4 * batch + 4):
            for half in range(2):
                source = half * N_Z + z_at(STEPS[j])
                at = 96 * j + 48 * half
                block = image[pl.ds(pl.multiple_of(source * OWN_ROWS, 16), OWN_ROWS), :]
                image_high[at : at + 48, :], image_low[at : at + 48, :] = split(block)

    def multiply(batch):
        span = slice(384 * batch, 384 * batch + 384)
        left = rows_turned[:, span]
        return dot(left, image_high[span, :]) + dot(left, image_low[span, :])

    split_image(0)
    split_image(1)
    for half in range(2):
        for dz in (3, -3):
            rows_landed(half * N_Z + z_at(dz))
        source = half * N_Z + z_at(4)
        landed(row_blocks.at[source, pl.ds(0, CUT)], row_recv.at[source, 0])
        landed(row_blocks.at[source, pl.ds(CUT, BLOCK - CUT)], row_recv.at[source, 1])
    turn_rows(1)
    pairs = multiply(0) + multiply(1)
    total = jnp.zeros((NT, 128), jnp.float32)
    for half in range(2):
        kept = jnp.zeros((NT, BOTH), jnp.float32)
        shared = base[NT * half : NT * half + NT, :]
        for l in range(NL):
            at = PAIRS * half + NT * l
            kept = jnp.where(lane_l == l, pairs[at : at + NT, :], kept)
        high, low = split(kept + shared)
        total = total + dot(high, fold[half]) + dot(low, fold[half])
    share = jnp.sum(jnp.where(band_lanes, total, 0.0), axis=0, keepdims=True)

    part_a[bulk] = share

    def others(number, own, step):
        repeat(0, number - 1, lambda k: step(jnp.where(k < own, k, k + 1)))

    others(BULK, bulk, lambda to: send(part_a.at[bulk], a_send, a_recv, to, wide))
    landed(parcels.at[pl.ds(0, 15)], parcel_send)
    landed(row_blocks.at[pl.ds(0, 15)], row_send)
    landed(part_a.at[pl.ds(0, BULK - 1)], a_recv)
    part_b[wide] = jnp.sum(part_a[...], axis=0)
    in_order = z * 2 + x_hi
    others(WIDE, in_order, lambda to: send(part_b.at[wide], b_send, b_recv, bulk, lax.rem(to, 2) * N_Z + lax.div(to, 2)))
    landed(part_a.at[pl.ds(0, BULK - 1)], a_send)
    landed(part_b.at[pl.ds(0, WIDE - 1)], b_recv)
    result = jnp.where(band_lanes, jnp.sum(part_b[...], axis=0), 0.0)
    lanes = iota((NT, 128), 1)
    for part in range(2):
        value = jnp.where(lax.div(lanes, 64) == part, result, 0.0)
        for shift in (8, 16, 32, 64):
            value = value + pltpu.roll(value, shift, 1)
        out_ref[part] = value[:, 0:NT]
    landed(part_b.at[pl.ds(0, WIDE - 1)], b_send)


def local(eps_corr, pair_rows, pair_cols, coulomb, wing_row, wing_col, pair_head, head_value, head_coulomb, inner_bands):
    bf16, f32 = jnp.bfloat16, jnp.float32
    dma = pltpu.SemaphoreType.DMA
    return pl.pallas_call(
        kernel,
        out_shape=jax.ShapeDtypeStruct((2, NT, NT), f32),
        in_specs=[pl.BlockSpec(memory_space=pltpu.HBM)] * 10,
        out_specs=pl.BlockSpec(memory_space=pltpu.VMEM),
        scratch_shapes=[
            pltpu.VMEM((UNITS, 2, ROWS, UNIT), bf16),
            pltpu.VMEM((2, OWN_ROWS, PAIRS), bf16),
            pltpu.VMEM((2, PAIRS, OWN), bf16),
            pltpu.VMEM((1, OWN), f32),
            pltpu.VMEM((2, OWN), bf16),
            pltpu.VMEM((2, OWN_ROWS), bf16),
            pltpu.VMEM((2, PAIRS), f32),
            pltpu.SMEM((2,), f32),
            pltpu.SMEM((1,), f32),
            pltpu.SMEM((NL,), jnp.int32),
            pltpu.VMEM((BULK, 288, 128), bf16),
            pltpu.VMEM((BOTH, OWN), bf16),
            pltpu.VMEM((WIDE, BLOCK, 128), bf16),
            pltpu.VMEM((ROWS, 256), bf16),
            pltpu.VMEM((BOTH, ROWS), bf16),
            pltpu.VMEM((BOTH, BOTH), bf16),
            pltpu.VMEM((2, BOTH, 128), bf16),
            pltpu.VMEM((ROWS, BOTH), f32),
            pltpu.VMEM((ROWS, BOTH), bf16),
            pltpu.VMEM((ROWS, BOTH), bf16),
            pltpu.VMEM((2 * NT, BOTH), f32),
            pltpu.VMEM((16, 1, 128), f32),
            pltpu.VMEM((16, 1, 128), f32),
            dma((UNITS,)),
            dma((9,)),
            dma,
            dma((BULK,)),
            dma,
            dma((WIDE, 2)),
            dma,
            dma,
            dma,
            dma,
        ],
        compiler_params=pltpu.CompilerParams(
            collective_id=0, has_side_effects=True, vmem_limit_bytes=63 * 1024 * 1024
        ),
    )(
        eps_corr,
        jnp.swapaxes(pair_rows, 1, 2),
        pair_cols,
        coulomb.reshape(1, OWN),
        wing_row,
        wing_col,
        pair_head,
        head_value,
        head_coulomb,
        inner_bands,
    )


def solution(mesh):
    placed = (
        P(None, "bulk", "wide"),
        P(None, None, ("bulk", "wide")),
        P(None, None, ("wide", "bulk")),
        P(("wide", "bulk")),
        P(None, ("wide", "bulk")),
        P(None, ("bulk", "wide")),
        P(),
        P(),
        P(),
        P(),
    )
    return jax.shard_map(local, mesh=mesh, in_specs=placed, out_specs=P(), check_vma=False)
```

time: 37.5 us -> 35.4 us (0.944)
  Pallas kernels: 35.4 us -> 33.3 us
    pallas_call x1, Pallas kernels: 35.4 us -> 33.3 us  [local(): pl.pallas_call(kernel, out_shape=jax.ShapeDtypeStruct((2, NT, NT), f32),...]
where the time goes in v3:
time: 35.4 us; the launch traced here: 35.3 us
  Pallas kernels  33.3 us (94%)
  local copies, waits for them, and re-layouts  1.3 us (4%)
  between operations  0.66 us (2%)
    pallas_call x1, Pallas kernels, local(): pl.pallas_call(kernel, out_shape=jax.ShapeDtypeStruct((2, NT, NT), f32),...  33.3 us
    unnamed x1, local copies, waits for them, and re-layouts  1.3 us

profile of v3, /device:TPU:1, one launch (start us, length us, event | category | flops | bytes accessed | tf_op | source)
XLA Modules:
  0.0 35.3 jit_solution(3612645686582107464)
XLA Ops:
  0.7 33.3 %shard_map.100 = f32[2,8,8]{2,1,0:T(8,128)} custom-call(bf16[2,768,3072]{2,1,0:T(8,128)(2,1)} %eps_hbm.1, bf16[2,48,96]{2,1,0:T(8,128)(2,1)} %bitcast.2, bf16[2,96,192]{2,1,0:T(8,128)(2,1)} %cols_hbm.1, f32[1,192]{1,0:T(1,128)} %bitcast.3, bf16[2,192]{1,0:T(2,128)(2,1)} %wing_row_hbm.1, bf16[2,48]{1,0:T(2,128)(2,1)} %wing_col_hbm.1, f32[2,96]{1,0:T(2,128)} %head_hbm.1, ...), custom_call_target="tpu_custom_call" | custom-call | tf_op jit(solution)/shard_map/pallas_call | solution.py:439
  34.0 1.3 %copy.13 = f32[2,8,8]{2,1,0:T(8,128)} copy(f32[2,8,8]{2,1,0:T(8,128)} %shard_map.100) | data formatting | bytes 1024

commit v4 on v3

--- a/solution.py
+++ b/solution.py
@@ -117,6 +117,25 @@
 
         lax.fori_loop(first, last, body, 0)
 
+    sibling = chip * 2 + 1 - core
+    across_x = lax.rem(x_hi + 1, 2) * N_Z + z
+
+    def along_z(dz):
+        return x_hi * N_Z + z_at(dz)
+
+    barrier = pltpu.get_barrier_semaphore()
+
+    def greet(to_bulk, to_wide):
+        pl.semaphore_signal(barrier, inc=1, device_id={"bulk": to_bulk, "wide": to_wide}, device_id_type=MESH)
+
+    greet(bulk, across_x)
+    greet(sibling, wide)
+    greet(across * 2 + core, wide)
+    for dy in (1, 3, 2):
+        greet(unit_at(0, dy) * 2 + core, wide)
+    for dz in (1, -1, 2, -2):
+        greet(bulk, along_z(dz))
+
     small = [
         pltpu.make_async_copy(src, dst, in_sem.at[i])
         for i, (src, dst) in enumerate(
@@ -133,33 +152,16 @@
             )
         )
     ]
-    for copy in small:
+    for copy in small[:3]:
         copy.start()
-
-    sibling = chip * 2 + 1 - core
-    across_x = lax.rem(x_hi + 1, 2) * N_Z + z
-
-    def along_z(dz):
-        return x_hi * N_Z + z_at(dz)
-
-    barrier = pltpu.get_barrier_semaphore()
-
-    def greet(to_bulk, to_wide):
-        pl.semaphore_signal(barrier, inc=1, device_id={"bulk": to_bulk, "wide": to_wide}, device_id_type=MESH)
-
-    greet(bulk, across_x)
-    greet(sibling, wide)
-    greet(across * 2 + core, wide)
-    for dy in (1, 3, 2):
-        greet(unit_at(0, dy) * 2 + core, wide)
-    for dz in (1, -1, 2, -2):
-        greet(bulk, along_z(dz))
 
     def slab(i):
         span = pl.ds(pl.multiple_of(unit_of(i) * UNIT, 128), UNIT)
         return pltpu.make_async_copy(eps_hbm.at[:, :, span], eps.at[i], eps_sem.at[i])
 
     repeat(0, UNITS, lambda i: slab(i).start())
+    for copy in small[3:]:
+        copy.start()
 
     pl.semaphore_wait(barrier, 10)
 
@@ -362,7 +364,7 @@
         def _():
             second_stage()
 
-        @pl.when(i == 5)
+        @pl.when(i == 3)
         def _():
             third_stage()
 
@@ -415,12 +417,12 @@
         repeat(0, number - 1, lambda k: step(jnp.where(k < own, k, k + 1)))
 
     others(BULK, bulk, lambda to: send(part_a.at[bulk], a_send, a_recv, to, wide))
-    landed(parcels.at[pl.ds(0, 15)], parcel_send)
-    landed(row_blocks.at[pl.ds(0, 15)], row_send)
     landed(part_a.at[pl.ds(0, BULK - 1)], a_recv)
     part_b[wide] = jnp.sum(part_a[...], axis=0)
     in_order = z * 2 + x_hi
     others(WIDE, in_order, lambda to: send(part_b.at[wide], b_send, b_recv, bulk, lax.rem(to, 2) * N_Z + lax.div(to, 2)))
+    landed(parcels.at[pl.ds(0, 15)], parcel_send)
+    landed(row_blocks.at[pl.ds(0, 15)], row_send)
     landed(part_a.at[pl.ds(0, BULK - 1)], a_send)
     landed(part_b.at[pl.ds(0, WIDE - 1)], b_recv)
     result = jnp.where(band_lanes, jnp.sum(part_b[...], axis=0), 0.0)

time: 35.4 us -> 34.9 us (0.986)
  Pallas kernels: 33.3 us -> 32.8 us
    pallas_call x1, Pallas kernels: 33.3 us -> 32.8 us  [local(): pl.pallas_call(kernel, out_shape=jax.ShapeDtypeStruct((2, NT, NT), f32),...]
where the time goes in v4:
time: 34.9 us; the launch traced here: 34.7 us
  Pallas kernels  32.8 us (94%)
  local copies, waits for them, and re-layouts  1.3 us (4%)
  between operations  0.66 us (2%)
    pallas_call x1, Pallas kernels, local(): pl.pallas_call(kernel, out_shape=jax.ShapeDtypeStruct((2, NT, NT), f32),...  32.8 us
    unnamed x1, local copies, waits for them, and re-layouts  1.3 us

profile of v4, /device:TPU:1, one launch (start us, length us, event | category | flops | bytes accessed | tf_op | source)
XLA Modules:
  0.0 34.7 jit_solution(10066187184243267106)
XLA Ops:
  0.7 32.8 %shard_map.100 = f32[2,8,8]{2,1,0:T(8,128)} custom-call(bf16[2,768,3072]{2,1,0:T(8,128)(2,1)} %eps_hbm.1, bf16[2,48,96]{2,1,0:T(8,128)(2,1)} %bitcast.2, bf16[2,96,192]{2,1,0:T(8,128)(2,1)} %cols_hbm.1, f32[1,192]{1,0:T(1,128)} %bitcast.3, bf16[2,192]{1,0:T(2,128)(2,1)} %wing_row_hbm.1, bf16[2,48]{1,0:T(2,128)(2,1)} %wing_col_hbm.1, f32[2,96]{1,0:T(2,128)} %head_hbm.1, ...), custom_call_target="tpu_custom_call" | custom-call | tf_op jit(solution)/shard_map/pallas_call | solution.py:441
  33.4 1.3 %copy.13 = f32[2,8,8]{2,1,0:T(8,128)} copy(f32[2,8,8]{2,1,0:T(8,128)} %shard_map.100) | data formatting | bytes 1024

commit v5 on v4

--- a/solution.py
+++ b/solution.py
@@ -115,7 +115,11 @@
             step(i)
             return carry
 
-        lax.fori_loop(first, last, body, 0)
+        if last - first > 4:
+            lax.fori_loop(first, last, body, 0)
+        else:
+            for i in range(first, last):
+                step(i)
 
     sibling = chip * 2 + 1 - core
     across_x = lax.rem(x_hi + 1, 2) * N_Z + z
@@ -224,7 +228,7 @@
 
     def send_along(of_wide):
         def step(i):
-            send_rows(of_wide, along_z(jnp.where(i < 2, i - 2, i - 1)))
+            send_rows(of_wide, along_z((2, -2, 1, -1)[i]))
 
         repeat(0, 4, step)
 

time: 34.9 us -> 34.8 us (level)
  no operation moved by 1% of the time
where the time goes in v5:
time: 34.8 us; the launch traced here: 34.6 us
  Pallas kernels  32.7 us (94%)
  local copies, waits for them, and re-layouts  1.3 us (4%)
  between operations  0.66 us (2%)
    pallas_call x1, Pallas kernels, local(): pl.pallas_call(kernel, out_shape=jax.ShapeDtypeStruct((2, NT, NT), f32),...  32.7 us
    unnamed x1, local copies, waits for them, and re-layouts  1.3 us

profile of v5, /device:TPU:1, one launch (start us, length us, event | category | flops | bytes accessed | tf_op | source)
XLA Modules:
  0.0 34.6 jit_solution(13128762790779108200)
XLA Ops:
  0.7 32.7 %shard_map.100 = f32[2,8,8]{2,1,0:T(8,128)} custom-call(bf16[2,768,3072]{2,1,0:T(8,128)(2,1)} %eps_hbm.1, bf16[2,48,96]{2,1,0:T(8,128)(2,1)} %bitcast.2, bf16[2,96,192]{2,1,0:T(8,128)(2,1)} %cols_hbm.1, f32[1,192]{1,0:T(1,128)} %bitcast.3, bf16[2,192]{1,0:T(2,128)(2,1)} %wing_row_hbm.1, bf16[2,48]{1,0:T(2,128)(2,1)} %wing_col_hbm.1, f32[2,96]{1,0:T(2,128)} %head_hbm.1, ...), custom_call_target="tpu_custom_call" | custom-call | tf_op jit(solution)/shard_map/pallas_call | solution.py:445
  33.3 1.3 %copy.13 = f32[2,8,8]{2,1,0:T(8,128)} copy(f32[2,8,8]{2,1,0:T(8,128)} %shard_map.100) | data formatting | bytes 1024

commit v6 on v5

--- a/solution.py
+++ b/solution.py
@@ -163,7 +163,6 @@
         span = pl.ds(pl.multiple_of(unit_of(i) * UNIT, 128), UNIT)
         return pltpu.make_async_copy(eps_hbm.at[:, :, span], eps.at[i], eps_sem.at[i])
 
-    repeat(0, UNITS, lambda i: slab(i).start())
     for copy in small[3:]:
         copy.start()
 
@@ -235,6 +234,7 @@
     send_along(wide)
     repeat(1, 4, lambda dy: relay(here, unit_at(0, dy)))
     hand_on(here)
+    repeat(0, UNITS, lambda i: slab(i).start())
 
     low_lanes = iota((PAIRS, 128), 1) < 64
 

time: 34.8 us -> 34.8 us (level)
  no operation moved by 1% of the time
where the time goes in v6:
time: 34.8 us; the launch traced here: 34.6 us
  Pallas kernels  32.7 us (94%)
  local copies, waits for them, and re-layouts  1.3 us (4%)
  between operations  0.66 us (2%)
    pallas_call x1, Pallas kernels, local(): pl.pallas_call(kernel, out_shape=jax.ShapeDtypeStruct((2, NT, NT), f32),...  32.7 us
    unnamed x1, local copies, waits for them, and re-layouts  1.3 us

profile of v6, /device:TPU:1, one launch (start us, length us, event | category | flops | bytes accessed | tf_op | source)
XLA Modules:
  0.0 34.6 jit_solution(3939727907537495852)
XLA Ops:
  0.7 32.7 %shard_map.100 = f32[2,8,8]{2,1,0:T(8,128)} custom-call(bf16[2,768,3072]{2,1,0:T(8,128)(2,1)} %eps_hbm.1, bf16[2,48,96]{2,1,0:T(8,128)(2,1)} %bitcast.2, bf16[2,96,192]{2,1,0:T(8,128)(2,1)} %cols_hbm.1, f32[1,192]{1,0:T(1,128)} %bitcast.3, bf16[2,192]{1,0:T(2,128)(2,1)} %wing_row_hbm.1, bf16[2,48]{1,0:T(2,128)(2,1)} %wing_col_hbm.1, f32[2,96]{1,0:T(2,128)} %head_hbm.1, ...), custom_call_target="tpu_custom_call" | custom-call | tf_op jit(solution)/shard_map/pallas_call | solution.py:445
  33.3 1.3 %copy.13 = f32[2,8,8]{2,1,0:T(8,128)} copy(f32[2,8,8]{2,1,0:T(8,128)} %shard_map.100) | data formatting | bytes 1024

commit v7 on v6

--- a/solution.py
+++ b/solution.py
@@ -319,7 +319,9 @@
         plain = jnp.concatenate([head_block, middle, tail_block], axis=1)
         turned = jnp.concatenate([-plain[PAIRS:], plain[:PAIRS]], axis=0)
         left = jnp.concatenate([eps[i, 0], eps[i, 1]], axis=1)
-        image[...] += dot_t(left, jnp.concatenate([plain, turned], axis=1))
+        right = jnp.concatenate([plain, turned], axis=1)
+        for at in range(0, ROWS, 256):
+            image[at : at + 256, :] += dot_t(left[at : at + 256], right)
 
     def relay_rows(at_x):
         for i, dz in enumerate((1, -1)):

time: 34.8 us -> 34.8 us (level)
  no operation moved by 1% of the time
where the time goes in v7:
time: 34.8 us; the launch traced here: 34.6 us
  Pallas kernels  32.7 us (94%)
  local copies, waits for them, and re-layouts  1.3 us (4%)
  between operations  0.66 us (2%)
    pallas_call x1, Pallas kernels, local(): pl.pallas_call(kernel, out_shape=jax.ShapeDtypeStruct((2, NT, NT), f32),...  32.7 us
    unnamed x1, local copies, waits for them, and re-layouts  1.3 us

profile of v7, /device:TPU:1, one launch (start us, length us, event | category | flops | bytes accessed | tf_op | source)
XLA Modules:
  0.0 34.6 jit_solution(2256819341656476276)
XLA Ops:
  0.7 32.7 %shard_map.100 = f32[2,8,8]{2,1,0:T(8,128)} custom-call(bf16[2,768,3072]{2,1,0:T(8,128)(2,1)} %eps_hbm.1, bf16[2,48,96]{2,1,0:T(8,128)(2,1)} %bitcast.2, bf16[2,96,192]{2,1,0:T(8,128)(2,1)} %cols_hbm.1, f32[1,192]{1,0:T(1,128)} %bitcast.3, bf16[2,192]{1,0:T(2,128)(2,1)} %wing_row_hbm.1, bf16[2,48]{1,0:T(2,128)(2,1)} %wing_col_hbm.1, f32[2,96]{1,0:T(2,128)} %head_hbm.1, ...), custom_call_target="tpu_custom_call" | custom-call | tf_op jit(solution)/shard_map/pallas_call | solution.py:447
  33.3 1.3 %copy.13 = f32[2,8,8]{2,1,0:T(8,128)} copy(f32[2,8,8]{2,1,0:T(8,128)} %shard_map.100) | data formatting | bytes 1024
